TPU v7x, 32 devices: a whole 2x2x4 slice. The times are simulated.
32 devices in a mesh: vessel: 4 (over x, core), blk: 8 (over z, y).
Axes of the slice: x: 2, y: 2, z: 4, core: 2. Of those that a mesh axis runs over, the one named last changes fastest.
Arguments:
- populations: float32 [19, 32, 256, 128], P(None, 'vessel', 'blk'), may hold values from 0.5 to 1.5
- voxel_mask: int32 [32, 256, 128], P('vessel', 'blk'), may hold values from 0 to 2
- tracer: float32 [64, 16, 128], P('blk', 'vessel'), may hold values from -6 to 6
Outputs:
- final_populations: float32 [19, 32, 256, 128], P(None, 'vessel', 'blk')
- final_tracer: float32 [64, 16, 128], P('blk', 'vessel')
All inputs are finite; a program needn't handle non-finite values.
Results may differ from a plain program's by a relative error of at most 0.0001.
Values sent between devices are 32-bit elements; how exact they have to be, the bound alone decides.
A program may use at most 128 MiB of HBM per device.

v0:
```python
import functools

import jax
import jax.numpy as jnp
import numpy as np
from jax import lax
from jax.experimental import pallas as pl
from jax.experimental.pallas import tpu as pltpu
from jax.sharding import PartitionSpec as P

STEPS = 4
TRACER_STEPS = 2

VELOCITY = [
    (0, 0, 0), (1, 0, 0), (-1, 0, 0), (0, 1, 0), (0, -1, 0), (0, 0, 1), (0, 0, -1),
    (1, 1, 0), (-1, -1, 0), (1, -1, 0), (-1, 1, 0), (1, 0, 1), (-1, 0, -1),
    (1, 0, -1), (-1, 0, 1), (0, 1, 1), (0, -1, -1), (0, 1, -1), (0, -1, 1),
]
PAIRS = [(i, i + 1) for i in range(1, 19, 2)]
ORDER = [9, 1, 11, 13, 7, 3, 15, 17, 10, 2, 12, 14, 8, 4, 16, 18, 0, 5, 6]
SLOT = {pop: k for k, pop in enumerate(ORDER)}
UP = [7, 3, 15, 17, 10]
DOWN = [8, 4, 16, 18, 9]
CORNERS = [(1, 1, 0, 0, 7), (-1, -1, 1, 0, 8), (1, -1, 1, 4, 9), (-1, 1, 0, 4, 10)]
AROUND = [(dx, dy) for dx in (-1, 0, 1) for dy in (-1, 0, 1) if (dx, dy) != (0, 0)]
MESH = pl.DeviceIdType.MESH
relax_rate = 1.25
pore_damping = 0.5
advect_gain = 8.0
diffusion = 0.1
ROW0 = 8


def moments(g):
    total = [g[i] + g[j] for i, j in PAIRS]
    diff = [g[i] - g[j] for i, j in PAIRS]
    axial = (total[0] + total[1]) + total[2]
    diagonal = ((total[3] + total[4]) + (total[5] + total[6])) + (total[7] + total[8])
    density = g[0] * (1.0 / 3.0) + axial * (1.0 / 18.0) + diagonal * (1.0 / 36.0)
    mom_x = diff[0] * (1.0 / 18.0) + ((diff[3] + diff[4]) + (diff[5] + diff[6])) * (1.0 / 36.0)
    mom_y = diff[1] * (1.0 / 18.0) + ((diff[3] - diff[4]) + (diff[7] + diff[8])) * (1.0 / 36.0)
    mom_z = diff[2] * (1.0 / 18.0) + ((diff[5] - diff[6]) + (diff[7] - diff[8])) * (1.0 / 36.0)
    return density, (mom_x, mom_y, mom_z)


def collide(g, mask):
    density, mom = moments(g)
    inverse = 1.0 / density
    factor = jnp.where(mask == 1, pore_damping * inverse, inverse)
    solid = mask == 2
    vel = [m * factor for m in mom]
    scaled = relax_rate * density
    speed_sq = vel[0] * vel[0] + vel[1] * vel[1] + vel[2] * vel[2]
    base = scaled * (1.0 - 1.5 * speed_sq)
    half = [1.5 * v for v in vel]
    linear = [(3.0 * scaled) * v for v in vel]
    keep = 1.0 - relax_rate
    post = [None] * 19
    post[0] = jnp.where(solid, g[0], base + keep * g[0])

    def along(comps, vec):
        total = None
        for c, v in zip(vec, comps):
            if c:
                part = v
                if total is None:
                    total = part if c > 0 else -part
                else:
                    total = total + part if c > 0 else total - part
        return total

    for i, j in PAIRS:
        proj = along(half, VELOCITY[i])
        odd = along(linear, VELOCITY[i])
        even = base + proj * odd
        post[i] = jnp.where(solid, g[j], (even + odd) + keep * g[i])
        post[j] = jnp.where(solid, g[i], (even - odd) + keep * g[j])
    return post


def kernel(sizes, names, pop_hbm, mask_hbm, tracer_ref, out_ref, conc_ref, pop, mask_ref, padded, ysend,
           yrecv, crecv, tracers, conc, flows, rows, coarse, gathered, load_sem, face_send, face_recv,
           tr_send, tr_recv, fl_send, fl_recv):
    vessels, blks, width, height, mz, my, reach = sizes
    tiles = height // 8
    own_rows = height // 2
    me_v = lax.axis_index(names[0])
    me_b = lax.axis_index(names[1])

    def at(dx, dy):
        return (lax.rem(me_v + dx + vessels, vessels), lax.rem(me_b + dy + blks, blks))

    last = width - 1
    spans = [(0, 1), (last, 1), (1, width - 2)]
    loads = [pltpu.make_async_copy(mask_hbm, mask_ref, load_sem.at[3])]
    for k, (start, count) in enumerate(spans):
        loads.append(
            pltpu.make_async_copy(
                pop_hbm.at[:, pl.ds(start, count)], pop.at[:, pl.ds(start, count)], load_sem.at[k]
            )
        )
    for load in loads:
        load.start()

    barrier = pltpu.get_barrier_semaphore()
    for dx in (-1, 0, 1):
        for k in range(blks):
            if dx == 0 and k == 0:
                continue
            pl.semaphore_signal(barrier, inc=1, device_id=at(dx, k), device_id_type=MESH)

    def gather(step, x, t):
        if step == 0:
            return [pop[i, x, pl.ds(8 * t, 8), :] for i in range(19)]
        g = []
        for i, (cx, cy, cz) in enumerate(VELOCITY):
            value = padded[step - 1, SLOT[i], x + 1 - cx, pl.ds(ROW0 + 8 * t - cy, 8), :]
            if cz:
                value = pltpu.roll(value, cz % 128, 1)
            g.append(value)
        return g

    def tile(step, x, t):
        g = gather(step, x, t)
        post = collide(g, mask_ref[x, pl.ds(8 * t, 8), :])
        for i in range(19):
            padded[step, SLOT[i], x + 1, pl.ds(ROW0 + 8 * t, 8), :] = post[i]
        if t == 0:
            for k, i in enumerate(DOWN):
                ysend[step, 1, k, pl.ds(x, 1), :] = post[i][0:1]
        if t == tiles - 1:
            for k, i in enumerate(UP):
                ysend[step, 0, k, pl.ds(x, 1), :] = post[i][7:8]

    def inner(step):
        def body(x, carry):
            for t in range(1, tiles - 1):
                tile(step, x, t)
            return carry

        lax.fori_loop(1, last, body, 0)

    def sides(step):
        def body(x, carry):
            tile(step, x, 0)
            tile(step, x, tiles - 1)
            return carry

        lax.fori_loop(1, last, body, 0)

    def ends(step):
        def body(k, carry):
            for t in range(tiles):
                tile(step, k * last, t)
            return carry

        lax.fori_loop(0, 2, body, 0)

    def copy(src, dst, send, recv, target):
        return pltpu.make_async_remote_copy(
            src_ref=src, dst_ref=dst, send_sem=send, recv_sem=recv, device_id=target, device_id_type=MESH
        )

    def x_copies(step):
        body = pl.ds(ROW0, height)
        found = []
        for k, (dx, first, plane, goal) in enumerate(((1, 0, width, 0), (-1, 8, 1, width + 1))):
            found.append(
                copy(
                    padded.at[step, pl.ds(first, 5), plane, body],
                    padded.at[step, pl.ds(first, 5), goal, body],
                    face_send.at[step, k], face_recv.at[step, k], at(dx, 0),
                )
            )
        return found

    def y_copies(step):
        found = []
        for k, dy in enumerate((1, -1)):
            found.append(
                copy(ysend.at[step, k], yrecv.at[step, k], face_send.at[step, 2 + k],
                     face_recv.at[step, 2 + k], at(0, dy))
            )
        for k, (dx, dy, which, place, _) in enumerate(CORNERS):
            found.append(
                copy(ysend.at[step, which, place], crecv.at[step, k], face_send.at[step, 4 + k],
                     face_recv.at[step, 4 + k], at(dx, dy))
            )
        return found

    def start(copies):
        for one in copies:
            one.start()

    def receive(step):
        beyond = ROW0 + height
        for one in y_copies(step):
            one.wait_recv()
        for x in range(width):
            for k in range(5):
                padded[step, SLOT[UP[k]], x + 1, pl.ds(ROW0 - 1, 1), :] = yrecv[step, 0, k, pl.ds(x, 1), :]
                padded[step, SLOT[DOWN[k]], x + 1, pl.ds(beyond, 1), :] = yrecv[step, 1, k, pl.ds(x, 1), :]
        for k, (dx, dy, _, _, i) in enumerate(CORNERS):
            row = ROW0 - 1 if dy == 1 else beyond
            plane, origin = (0, last) if dx == 1 else (width + 1, 0)
            padded[step, SLOT[i], plane, pl.ds(row, 1), :] = crecv[step, k, pl.ds(origin, 1), :]
        for one in x_copies(step):
            one.wait_recv()

    tr_copies = []
    for k, (dx, dy) in enumerate(AROUND):
        if dy == 0:
            src, goal = tracer_ref, pl.ds(2, mz)
        elif dy == 1:
            src, goal = tracer_ref.at[pl.ds(mz - 2, 2)], pl.ds(0, 2)
        else:
            src, goal = tracer_ref.at[pl.ds(0, 2)], pl.ds(mz + 2, 2)
        tr_copies.append(
            copy(src, tracers.at[1 - dx, goal], tr_send.at[k], tr_recv.at[k], at(dx, dy))
        )

    loads[0].wait()
    loads[1].wait()
    loads[2].wait()
    ends(0)
    pl.semaphore_wait(barrier, 3 * blks - 1)
    sent = x_copies(0)
    start(sent)
    loads[3].wait()
    sides(0)
    pending = y_copies(0)
    start(pending)
    start(tr_copies)
    sent += pending + tr_copies
    inner(0)
    tracers[1, pl.ds(2, mz)] = tracer_ref[...]
    for step in range(1, STEPS):
        inner(step)
        receive(step - 1)
        ends(step)
        pending = x_copies(step)
        start(pending)
        sent += pending
        sides(step)
        pending = y_copies(step)
        start(pending)
        sent += pending

    count = blks * reach
    line = lax.broadcasted_iota(jnp.int32, (count, 128), 0)
    cell = lax.shift_right_logical(lax.broadcasted_iota(jnp.int32, (count, 128), 1), 1)
    owner = lax.shift_right_logical(line, int(np.log2(reach)))
    offset = line - owner * reach
    wanted = owner * mz - 2 + offset
    wanted = jnp.where(wanted < 0, wanted + mz * blks, wanted)
    wanted = jnp.where(wanted >= mz * blks, wanted - mz * blks, wanted)
    spread = jnp.where((wanted == cell) & (offset < mz + 4), jnp.float32(0.125), jnp.float32(0.0))

    for one in tr_copies:
        one.wait_recv()
    conc[...] = jnp.zeros(conc.shape, jnp.float32)
    for a in range(8):
        if a < 2:
            side, cut = 0, a + 2
        elif a < 6:
            side, cut = 1, a - 2
        else:
            side, cut = 2, a - 6
        for j in range(mz + 4):
            conc[a, pl.ds(j, 1), :] = tracers[side, j, pl.ds(cut, 1), :]

    def finish(pair, t):
        sums = None
        for half in range(2):
            x = 2 * pair + half
            g = gather(STEPS, x, t)
            for i in range(19):
                out_ref[i, x, pl.ds(8 * t, 8), :] = g[i]
            density, mom = moments(g)
            inverse = jnp.where(mask_ref[x, pl.ds(8 * t, 8), :] == 2, 0.0, 1.0 / density)
            flow = [m * inverse for m in mom]
            sums = flow if sums is None else [a + b for a, b in zip(sums, flow)]
        for c in range(3):
            flows[c, pair, pl.ds(8 * t, 8), :] = sums[c]

    pairs = width // 2

    def middle(pair, carry):
        for t in range(1, tiles - 1):
            finish(pair, t)
        return carry

    def edges(pair, carry):
        finish(pair, 0)
        finish(pair, tiles - 1)
        return carry

    lax.fori_loop(1, pairs - 1, middle, 0)
    rows[...] = jnp.zeros(rows.shape, jnp.float32)
    receive(STEPS - 1)
    lax.fori_loop(1, pairs - 1, edges, 0)

    def outer(k, carry):
        for t in range(tiles):
            finish(k * (pairs - 1), t)
        return carry

    lax.fori_loop(0, 2, outer, 0)
    for p in range(2):
        for c in range(3):
            for xi in range(2):
                even = flows[c, 2 * p + xi, pl.ds(0, own_rows, 2), :]
                odd = flows[c, 2 * p + xi, pl.ds(1, own_rows, 2), :]
                rows[p, pl.ds((2 * c + xi) * own_rows, own_rows), :] = even + odd
        laid = lax.dot_general(
            spread, rows[p], (((1,), (1,)), ((), ())),
            precision=lax.Precision.HIGHEST, preferred_element_type=jnp.float32,
        )
        for b in range(blks):
            coarse[b, p] = laid[b * reach : (b + 1) * reach]

    def flow_copy(dx, goal_blk, from_blk):
        if dx == 0:
            src, dst = coarse.at[goal_blk], gathered.at[1, from_blk]
        else:
            part = 1 if dx == 1 else 0
            src, dst = coarse.at[goal_blk, part], gathered.at[1 - dx, from_blk, part]
        return copy(
            src, dst, fl_send.at[1 + dx, goal_blk], fl_recv.at[1 - dx, from_blk],
            (lax.rem(me_v + dx + vessels, vessels), goal_blk),
        )

    for k in range(blks):
        for dx in (1, -1, 0):
            if dx == 0 and k == 0:
                continue
            one = flow_copy(dx, lax.rem(me_b + k, blks), me_b)
            one.start()
            sent.append(one)
    gathered[1, me_b] = coarse[me_b]
    for one in sent:
        one.wait_send()
    for k in range(blks):
        for dx in (1, -1, 0):
            if dx == 0 and k == 0:
                continue
            flow_copy(dx, me_b, lax.rem(me_b + k, blks)).wait_recv()

    group = lax.shift_right_logical(lax.broadcasted_iota(jnp.int32, (reach, 128), 1), 4)
    flow = [[None] * 8 for _ in range(3)]
    for pair in range(4):
        side, part = ((0, 1), (1, 0), (1, 1), (2, 0))[pair]
        for c in range(3):
            for xi in range(2):
                place = 2 * c + xi
                lanes = []
                for tile_at in range(my // 128):
                    total = None
                    for b in range(8):
                        piece = gathered[side, tile_at * 8 + b, part]
                        shift = ((b - place) * 16) % 128
                        if shift:
                            piece = pltpu.roll(piece, shift, 1)
                        total = piece if total is None else jnp.where(group == b, piece, total)
                    lanes.append(total)
                flow[c][2 * pair + xi] = lanes[0] if len(lanes) == 1 else jnp.concatenate(lanes, axis=1)

    now = [conc[a] for a in range(8)]
    for step in range(TRACER_STEPS):
        new = list(now)
        for a in range(1 + step, 7 - step):
            here = now[a]
            flux_y = flow[1][a] * here
            flux_z = flow[2][a] * here
            div = (
                (flow[0][a + 1] * now[a + 1] - flow[0][a - 1] * now[a - 1])
                + (pltpu.roll(flux_y, my - 1, 1) - pltpu.roll(flux_y, 1, 1))
                + (pltpu.roll(flux_z, reach - 1, 0) - pltpu.roll(flux_z, 1, 0))
            ) * 0.5
            beside = (
                (now[a + 1] + now[a - 1])
                + (pltpu.roll(here, my - 1, 1) + pltpu.roll(here, 1, 1))
                + (pltpu.roll(here, reach - 1, 0) + pltpu.roll(here, 1, 0))
            )
            new[a] = here - advect_gain * div + diffusion * (beside - 6.0 * here)
        now = new
    for a in range(4):
        for j in range(mz):
            conc_ref[j, pl.ds(a, 1), :] = now[a + 2][j + 2 : j + 3]


def solution(mesh):
    names = ("vessel", "blk")
    vessels, blks = mesh.shape["vessel"], mesh.shape["blk"]

    def local(populations, voxel_mask, tracer):
        _, width, height, _ = populations.shape
        mz, mx, my = tracer.shape
        reach = 8 * (-(-(mz + 4) // 8))
        sizes = (vessels, blks, width, height, mz, my, reach)
        vmem = pl.BlockSpec(memory_space=pltpu.VMEM)
        hbm = pl.BlockSpec(memory_space=pl.ANY)
        f32 = jnp.float32
        dma = pltpu.SemaphoreType.DMA
        return pl.pallas_call(
            functools.partial(kernel, sizes, names),
            out_shape=(
                jax.ShapeDtypeStruct(populations.shape, f32),
                jax.ShapeDtypeStruct(tracer.shape, f32),
            ),
            in_specs=[hbm, hbm, vmem],
            out_specs=(vmem, vmem),
            scratch_shapes=[
                pltpu.VMEM(populations.shape, f32),
                pltpu.VMEM(voxel_mask.shape, jnp.int32),
                pltpu.VMEM((STEPS, 19, width + 2, height + 16, 128), f32),
                pltpu.VMEM((STEPS, 2, 5, width, 128), f32),
                pltpu.VMEM((STEPS, 2, 5, width, 128), f32),
                pltpu.VMEM((STEPS, 4, width, 128), f32),
                pltpu.VMEM((3, mz + 4, mx, my), f32),
                pltpu.VMEM((8, reach, my), f32),
                pltpu.VMEM((3, width // 2, height, 128), f32),
                pltpu.VMEM((2, 128, 128), f32),
                pltpu.VMEM((blks, 2, reach, 128), f32),
                pltpu.VMEM((3, blks, 2, reach, 128), f32),
                dma((4,)),
                dma((STEPS, 8)),
                dma((STEPS, 8)),
                dma((8,)),
                dma((8,)),
                dma((3, blks)),
                dma((3, blks)),
            ],
            compiler_params=pltpu.CompilerParams(
                collective_id=0, has_side_effects=True, vmem_limit_bytes=48 * 1024 * 1024
            ),
        )(populations, voxel_mask, tracer)

    return jax.shard_map(
        local,
        mesh=mesh,
        in_specs=(P(None, "vessel", "blk", None), P("vessel", "blk", None), P("blk", "vessel", None)),
        out_specs=(P(None, "vessel", "blk", None), P("blk", "vessel", None)),
        check_vma=False,
    )
```

profile of v0, /device:TPU:0, one launch (start us, length us, event | category | flops | bytes accessed | tf_op | source)
XLA Modules:
  0.0 42.0 jit_solution(12181576848992679952)
XLA Ops:
  0.6 0.0 copy-start
  0.6 1.7 %copy-done = f32[19,8,32,128]{3,2,1,0:T(8,128)S(1)} copy-done((f32[19,8,32,128]{3,2,1,0:T(8,128)S(1)}, f32[19,8,32,128]{3,2,1,0:T(8,128)}, u32[]{:S(2)}) %copy-start) | copy-done | bytes 2490392
  2.3 0.0 copy-start.1
  2.3 0.9 %copy-done.1 = s32[8,32,128]{2,1,0:T(8,128)S(1)} copy-done((s32[8,32,128]{2,1,0:T(8,128)S(1)}, s32[8,32,128]{2,1,0:T(8,128)}, u32[]{:S(2)}) %copy-start.1) | copy-done | bytes 131096
  3.2 0.0 copy-start.2
  3.2 0.7 %copy-done.2 = f32[8,4,128]{2,1,0:T(4,128)S(1)} copy-done((f32[8,4,128]{2,1,0:T(4,128)S(1)}, f32[8,4,128]{2,1,0:T(4,128)}, u32[]{:S(2)}) %copy-start.2) | copy-done | bytes 16408
  4.0 36.0 %shard_map.50 = (f32[19,8,32,128]{3,2,1,0:T(8,128)S(1)}, f32[8,4,128]{2,1,0:T(4,128)S(1)}) custom-call(f32[19,8,32,128]{3,2,1,0:T(8,128)S(1)} %copy-done, s32[8,32,128]{2,1,0:T(8,128)S(1)} %copy-done.1, f32[8,4,128]{2,1,0:T(4,128)S(1)} %copy-done.2), custom_call_target="tpu_custom_call" | custom-call | tf_op jit(solution)/shard_map/pallas_call | solution.py:405
  39.9 1.5 %copy.7 = f32[19,8,32,128]{3,2,1,0:T(8,128)} copy(f32[19,8,32,128]{3,2,1,0:T(8,128)S(1)} %get-tuple-element.4) | data formatting | bytes 4980736
  41.4 0.6 %copy.8 = f32[8,4,128]{2,1,0:T(4,128)} copy(f32[8,4,128]{2,1,0:T(4,128)S(1)} %get-tuple-element.5) | data formatting | bytes 32768
Async XLA Ops:
  0.6 1.7 %copy-start = (f32[19,8,32,128]{3,2,1,0:T(8,128)S(1)}, f32[19,8,32,128]{3,2,1,0:T(8,128)}, u32[]{:S(2)}) copy-start(f32[19,8,32,128]{3,2,1,0:T(8,128)} %pop_hbm.1) | copy-start | bytes 7471108
  2.3 0.9 %copy-start.1 = (s32[8,32,128]{2,1,0:T(8,128)S(1)}, s32[8,32,128]{2,1,0:T(8,128)}, u32[]{:S(2)}) copy-start(s32[8,32,128]{2,1,0:T(8,128)} %mask_hbm.1) | copy-start | bytes 393220
  3.2 0.7 %copy-start.2 = (f32[8,4,128]{2,1,0:T(4,128)S(1)}, f32[8,4,128]{2,1,0:T(4,128)}, u32[]{:S(2)}) copy-start(f32[8,4,128]{2,1,0:T(4,128)} %tracer_ref.1) | copy-start | bytes 49156
where the time goes:
time: 42.2 us; the launch traced here: 42 us
  Pallas kernels  36 us (85%)
  local copies, waits for them, and re-layouts  5.37 us (13%)
  between operations  0.65 us (2%)
    pallas_call x1, Pallas kernels, local(): pl.pallas_call(functools.partial(kernel, sizes, names), out_shape=(jax.Sh...  36 us
    unnamed x8, local copies, waits for them, and re-layouts  5.37 us

commit v1 on v0

--- a/solution.py
+++ b/solution.py
@@ -78,11 +78,12 @@
     return post
 
 
-def kernel(sizes, names, pop_hbm, mask_hbm, tracer_ref, out_ref, conc_ref, pop, mask_ref, padded, ysend,
+def kernel(sizes, names, pop_hbm, mask_hbm, tracer_hbm, out_ref, conc_ref, pop, mask_ref, padded, ysend,
            yrecv, crecv, tracers, conc, flows, rows, coarse, gathered, load_sem, face_send, face_recv,
            tr_send, tr_recv, fl_send, fl_recv):
     vessels, blks, width, height, mz, my, reach = sizes
     tiles = height // 8
+    pitch = height + 16
     own_rows = height // 2
     me_v = lax.axis_index(names[0])
     me_b = lax.axis_index(names[1])
@@ -99,6 +100,7 @@
                 pop_hbm.at[:, pl.ds(start, count)], pop.at[:, pl.ds(start, count)], load_sem.at[k]
             )
         )
+    loads.append(pltpu.make_async_copy(tracer_hbm, tracers.at[1, pl.ds(2, mz)], load_sem.at[4]))
     for load in loads:
         load.start()
 
@@ -125,12 +127,26 @@
         post = collide(g, mask_ref[x, pl.ds(8 * t, 8), :])
         for i in range(19):
             padded[step, SLOT[i], x + 1, pl.ds(ROW0 + 8 * t, 8), :] = post[i]
-        if t == 0:
-            for k, i in enumerate(DOWN):
-                ysend[step, 1, k, pl.ds(x, 1), :] = post[i][0:1]
-        if t == tiles - 1:
-            for k, i in enumerate(UP):
-                ysend[step, 0, k, pl.ds(x, 1), :] = post[i][7:8]
+
+    flat = padded.reshape(STEPS, 19, (width + 2) * pitch, 128)
+    flat_pop = pop.reshape(19, width * height, 128)
+    flat_mask = mask_ref.reshape(width * height, 128)
+
+    def border(step):
+        for which, y, names_of in ((1, 0, DOWN), (0, height - 1, UP)):
+            if step == 0:
+                g = [flat_pop[i, pl.ds(y, width, height), :] for i in range(19)]
+            else:
+                g = []
+                for i, (cx, cy, cz) in enumerate(VELOCITY):
+                    begin = (1 - cx) * pitch + ROW0 + y - cy
+                    value = flat[step - 1, SLOT[i], pl.ds(begin, width, pitch), :]
+                    if cz:
+                        value = pltpu.roll(value, cz % 128, 1)
+                    g.append(value)
+            post = collide(g, flat_mask[pl.ds(y, width, height), :])
+            for k, i in enumerate(names_of):
+                ysend[step, which, k] = post[i]
 
     def inner(step):
         def body(x, carry):
@@ -196,10 +212,9 @@
         beyond = ROW0 + height
         for one in y_copies(step):
             one.wait_recv()
-        for x in range(width):
-            for k in range(5):
-                padded[step, SLOT[UP[k]], x + 1, pl.ds(ROW0 - 1, 1), :] = yrecv[step, 0, k, pl.ds(x, 1), :]
-                padded[step, SLOT[DOWN[k]], x + 1, pl.ds(beyond, 1), :] = yrecv[step, 1, k, pl.ds(x, 1), :]
+        for k in range(5):
+            flat[step, SLOT[UP[k]], pl.ds(pitch + ROW0 - 1, width, pitch), :] = yrecv[step, 0, k]
+            flat[step, SLOT[DOWN[k]], pl.ds(pitch + beyond, width, pitch), :] = yrecv[step, 1, k]
         for k, (dx, dy, _, _, i) in enumerate(CORNERS):
             row = ROW0 - 1 if dy == 1 else beyond
             plane, origin = (0, last) if dx == 1 else (width + 1, 0)
@@ -210,13 +225,13 @@
     tr_copies = []
     for k, (dx, dy) in enumerate(AROUND):
         if dy == 0:
-            src, goal = tracer_ref, pl.ds(2, mz)
+            src, goal = pl.ds(2, mz), pl.ds(2, mz)
         elif dy == 1:
-            src, goal = tracer_ref.at[pl.ds(mz - 2, 2)], pl.ds(0, 2)
+            src, goal = pl.ds(mz, 2), pl.ds(0, 2)
         else:
-            src, goal = tracer_ref.at[pl.ds(0, 2)], pl.ds(mz + 2, 2)
+            src, goal = pl.ds(2, 2), pl.ds(mz + 2, 2)
         tr_copies.append(
-            copy(src, tracers.at[1 - dx, goal], tr_send.at[k], tr_recv.at[k], at(dx, dy))
+            copy(tracers.at[1, src], tracers.at[1 - dx, goal], tr_send.at[k], tr_recv.at[k], at(dx, dy))
         )
 
     loads[0].wait()
@@ -227,24 +242,26 @@
     sent = x_copies(0)
     start(sent)
     loads[3].wait()
-    sides(0)
+    border(0)
     pending = y_copies(0)
     start(pending)
+    sides(0)
+    loads[4].wait()
     start(tr_copies)
     sent += pending + tr_copies
     inner(0)
-    tracers[1, pl.ds(2, mz)] = tracer_ref[...]
     for step in range(1, STEPS):
         inner(step)
         receive(step - 1)
+        border(step)
+        pending = y_copies(step)
+        start(pending)
+        sent += pending
         ends(step)
         pending = x_copies(step)
         start(pending)
         sent += pending
         sides(step)
-        pending = y_copies(step)
-        start(pending)
-        sent += pending
 
     count = blks * reach
     line = lax.broadcasted_iota(jnp.int32, (count, 128), 0)
@@ -399,7 +416,7 @@
         reach = 8 * (-(-(mz + 4) // 8))
         sizes = (vessels, blks, width, height, mz, my, reach)
         vmem = pl.BlockSpec(memory_space=pltpu.VMEM)
-        hbm = pl.BlockSpec(memory_space=pl.ANY)
+        hbm = pl.BlockSpec(memory_space=pltpu.HBM)
         f32 = jnp.float32
         dma = pltpu.SemaphoreType.DMA
         return pl.pallas_call(
@@ -408,7 +425,7 @@
                 jax.ShapeDtypeStruct(populations.shape, f32),
                 jax.ShapeDtypeStruct(tracer.shape, f32),
             ),
-            in_specs=[hbm, hbm, vmem],
+            in_specs=[hbm, hbm, hbm],
             out_specs=(vmem, vmem),
             scratch_shapes=[
                 pltpu.VMEM(populations.shape, f32),
@@ -423,7 +440,7 @@
                 pltpu.VMEM((2, 128, 128), f32),
                 pltpu.VMEM((blks, 2, reach, 128), f32),
                 pltpu.VMEM((3, blks, 2, reach, 128), f32),
-                dma((4,)),
+                dma((5,)),
                 dma((STEPS, 8)),
                 dma((STEPS, 8)),
                 dma((8,)),
@@ -432,7 +449,7 @@
                 dma((3, blks)),
             ],
             compiler_params=pltpu.CompilerParams(
-                collective_id=0, has_side_effects=True, vmem_limit_bytes=48 * 1024 * 1024
+                collective_id=0, has_side_effects=True, vmem_limit_bytes=54 * 1024 * 1024
             ),
         )(populations, voxel_mask, tracer)
 

time: 42.2 us -> 38 us (0.900)
  Pallas kernels: 36 us -> 33.1 us
  local copies, waits for them, and re-layouts: 5.37 us -> 4.09 us
    pallas_call x1, Pallas kernels: 36 us -> 33.1 us  [local(): pl.pallas_call(functools.partial(kernel, sizes, names), out_shape=(jax.Sh...]
    unnamed x8 -> x4, local copies, waits for them, and re-layouts: 5.37 us -> 4.09 us
where the time goes in v1:
time: 38 us; the launch traced here: 37.8 us
  Pallas kernels  33.1 us (87%)
  local copies, waits for them, and re-layouts  4.09 us (11%)
  between operations  0.65 us (2%)
    pallas_call x1, Pallas kernels, local(): pl.pallas_call(functools.partial(kernel, sizes, names), out_shape=(jax.Sh...  33.1 us
    unnamed x4, local copies, waits for them, and re-layouts  4.09 us

profile of v1, /device:TPU:0, one launch (start us, length us, event | category | flops | bytes accessed | tf_op | source)
XLA Modules:
  0.0 37.8 jit_solution(14115853838400942513)
XLA Ops:
  0.6 33.1 %shard_map.50 = (f32[19,8,32,128]{3,2,1,0:T(8,128)}, f32[8,4,128]{2,1,0:T(4,128)}) custom-call(f32[19,8,32,128]{3,2,1,0:T(8,128)} %pop_hbm.1, s32[8,32,128]{2,1,0:T(8,128)} %mask_hbm.1, f32[8,4,128]{2,1,0:T(4,128)} %tracer_hbm.1), custom_call_target="tpu_custom_call" | custom-call | tf_op jit(solution)/shard_map/pallas_call | solution.py:422
  33.7 0.0 copy-start
  33.7 3.5 %copy.7 = f32[19,8,32,128]{3,2,1,0:T(8,128)} copy(f32[19,8,32,128]{3,2,1,0:T(8,128)} %get-tuple-element.4) | data formatting | bytes 4980736
  37.2 0.0 copy-done
  37.2 0.6 %copy.8 = f32[8,4,128]{2,1,0:T(4,128)} copy(f32[8,4,128]{2,1,0:T(4,128)S(1)} %copy-done) | data formatting | bytes 32768
Async XLA Ops:
  33.7 3.5 %copy-start = (f32[8,4,128]{2,1,0:T(4,128)S(1)}, f32[8,4,128]{2,1,0:T(4,128)}, u32[]{:S(2)}) copy-start(f32[8,4,128]{2,1,0:T(4,128)} %get-tuple-element.5) | copy-start | bytes 49156

commit v2 on v1

--- a/solution.py
+++ b/solution.py
@@ -237,14 +237,14 @@
     loads[0].wait()
     loads[1].wait()
     loads[2].wait()
+    loads[3].wait()
+    border(0)
+    pl.semaphore_wait(barrier, 3 * blks - 1)
+    pending = y_copies(0)
+    start(pending)
     ends(0)
-    pl.semaphore_wait(barrier, 3 * blks - 1)
     sent = x_copies(0)
     start(sent)
-    loads[3].wait()
-    border(0)
-    pending = y_copies(0)
-    start(pending)
     sides(0)
     loads[4].wait()
     start(tr_copies)
@@ -291,8 +291,6 @@
         for half in range(2):
             x = 2 * pair + half
             g = gather(STEPS, x, t)
-            for i in range(19):
-                out_ref[i, x, pl.ds(8 * t, 8), :] = g[i]
             density, mom = moments(g)
             inverse = jnp.where(mask_ref[x, pl.ds(8 * t, 8), :] == 2, 0.0, 1.0 / density)
             flow = [m * inverse for m in mom]
@@ -355,6 +353,15 @@
             one.start()
             sent.append(one)
     gathered[1, me_b] = coarse[me_b]
+
+    def emit(x, carry):
+        for t in range(tiles):
+            g = gather(STEPS, x, t)
+            for i in range(19):
+                out_ref[i, x, pl.ds(8 * t, 8), :] = g[i]
+        return carry
+
+    lax.fori_loop(0, width, emit, 0)
     for one in sent:
         one.wait_send()
     for k in range(blks):
@@ -449,7 +456,7 @@
                 dma((3, blks)),
             ],
             compiler_params=pltpu.CompilerParams(
-                collective_id=0, has_side_effects=True, vmem_limit_bytes=54 * 1024 * 1024
+                collective_id=0, has_side_effects=True, vmem_limit_bytes=51 * 1024 * 1024
             ),
         )(populations, voxel_mask, tracer)
 

time: 38 us -> 36.7 us (0.966)
  Pallas kernels: 33.1 us -> 32.1 us
  local copies, waits for them, and re-layouts: 4.09 us -> 3.67 us
    pallas_call x1, Pallas kernels: 33.1 us -> 32.1 us  [local(): pl.pallas_call(functools.partial(kernel, sizes, names), out_shape=(jax.Sh...]
    unnamed x4 -> x6, local copies, waits for them, and re-layouts: 4.09 us -> 3.67 us
where the time goes in v2:
time: 36.7 us; the launch traced here: 36.4 us
  Pallas kernels  32.1 us (87%)
  local copies, waits for them, and re-layouts  3.67 us (10%)
  between operations  0.65 us (2%)
    pallas_call x1, Pallas kernels, local(): pl.pallas_call(functools.partial(kernel, sizes, names), out_shape=(jax.Sh...  32.1 us
    unnamed x6, local copies, waits for them, and re-layouts  3.67 us

profile of v2, /device:TPU:0, one launch (start us, length us, event | category | flops | bytes accessed | tf_op | source)
XLA Modules:
  0.0 36.4 jit_solution(15570938750004820815)
XLA Ops:
  0.6 0.0 copy-start
  0.6 0.9 %copy-done = s32[8,32,128]{2,1,0:T(8,128)S(1)} copy-done((s32[8,32,128]{2,1,0:T(8,128)S(1)}, s32[8,32,128]{2,1,0:T(8,128)}, u32[]{:S(2)}) %copy-start) | copy-done | bytes 131096
  1.5 0.0 copy-start.1
  1.5 0.7 %copy-done.1 = f32[8,4,128]{2,1,0:T(4,128)S(1)} copy-done((f32[8,4,128]{2,1,0:T(4,128)S(1)}, f32[8,4,128]{2,1,0:T(4,128)}, u32[]{:S(2)}) %copy-start.1) | copy-done | bytes 16408
  2.3 32.1 %shard_map.50 = (f32[19,8,32,128]{3,2,1,0:T(8,128)S(1)}, f32[8,4,128]{2,1,0:T(4,128)S(1)}) custom-call(f32[19,8,32,128]{3,2,1,0:T(8,128)} %pop_hbm.1, s32[8,32,128]{2,1,0:T(8,128)S(1)} %copy-done, f32[8,4,128]{2,1,0:T(4,128)S(1)} %copy-done.1), custom_call_target="tpu_custom_call" | custom-call | tf_op jit(solution)/shard_map/pallas_call | solution.py:429
  34.4 1.5 %copy.7 = f32[19,8,32,128]{3,2,1,0:T(8,128)} copy(f32[19,8,32,128]{3,2,1,0:T(8,128)S(1)} %get-tuple-element.4) | data formatting | bytes 4980736
  35.8 0.6 %copy.8 = f32[8,4,128]{2,1,0:T(4,128)} copy(f32[8,4,128]{2,1,0:T(4,128)S(1)} %get-tuple-element.5) | data formatting | bytes 32768
Async XLA Ops:
  0.6 0.9 %copy-start = (s32[8,32,128]{2,1,0:T(8,128)S(1)}, s32[8,32,128]{2,1,0:T(8,128)}, u32[]{:S(2)}) copy-start(s32[8,32,128]{2,1,0:T(8,128)} %mask_hbm.1) | copy-start | bytes 393220
  1.5 0.7 %copy-start.1 = (f32[8,4,128]{2,1,0:T(4,128)S(1)}, f32[8,4,128]{2,1,0:T(4,128)}, u32[]{:S(2)}) copy-start(f32[8,4,128]{2,1,0:T(4,128)} %tracer_hbm.1) | copy-start | bytes 49156
